TPU v7x, 256 devices: a whole 4x4x8 slice. The times are simulated.
256 devices in a mesh: row: 32 (over y, x, core), col: 8 (over z).
Axes of the slice: x: 4, y: 4, z: 8, core: 2. Of those that a mesh axis runs over, the one named last changes fastest.
Arguments:
- objective: float32 [16384, 2048], P('row', 'col'), may hold values from -6 to 6
- pivots: int32 [16384], P('row'), may hold values from 0 to 16383, as said below
- panel: float32 [16384, 1024], P('row', 'col'), as said below
Outputs:
- reduced: float32 [16384, 2048], P('row', 'col')
Inputs may be any that keep to these rules, and one draw needn't show every extreme that they name: `pivots`: row b * 512 + o of the pivoted order takes objective row ((b + s_o) mod 32) * 512 + t_o, where o -> t_o is a permutation of 0 to 511 and the shift s_o depends on o alone; every shift from 1 to 31 is taken by exactly 8 offsets, shift 0 by the others. Each tile on the diagonal is lower triangular with diagonal entries between 2 and 4; entries above the diagonal of the whole panel are zero.
All inputs are finite; a program needn't handle non-finite values.
Results may differ from a plain program's by a relative error of at most 0.00013.
Values sent between devices are 32-bit elements; how exact they have to be, the bound alone decides.
A program may use at most 64 MiB of HBM per device.

v0:
```python
import jax
import jax.numpy as jnp
from jax import lax
from jax.sharding import PartitionSpec as P

N = 16384
NB = 512
PANELS = 2
CAP = 8


def from_root(block, axis, holder):
    block = jnp.where(lax.axis_index(axis) == holder, block, jnp.zeros_like(block))
    return lax.psum(block, axis)


def body(objective, pivots, panel):
    row_count = objective.shape[0]
    col_count = objective.shape[1]
    block_here = row_count // NB
    block_count = N // NB
    spare_count = NB - CAP * (block_count - 1)
    device_count = lax.axis_size("row")
    my_index = lax.axis_index("row")
    first_block = my_index * block_here
    block_shift = (pivots // NB - first_block) % block_count
    within_block = pivots % NB
    shift_order = jnp.argsort(block_shift, stable=True)
    shift_rank = jnp.argsort(shift_order, stable=True)
    offset_table = shift_order[spare_count:].reshape(block_count - 1, CAP)
    dest_device = jnp.arange(device_count, dtype=jnp.int32)[:, None, None]
    dest_local = jnp.arange(block_here, dtype=jnp.int32)[None, :, None]
    source_local = jnp.arange(block_here, dtype=jnp.int32)[None, None, :]
    needed_shift = (
        first_block + source_local - dest_device * block_here - dest_local
    ) % block_count
    picked_offsets = offset_table[jnp.maximum(needed_shift, 1) - 1]
    send_rows = source_local[..., None] * NB + within_block[picked_offsets]
    outgoing = objective[send_rows]
    incoming = lax.all_to_all(outgoing, "row", split_axis=0, concat_axis=0, tiled=True)
    flat_incoming = incoming.reshape(-1, col_count)
    own_local = jnp.arange(block_here, dtype=jnp.int32)[:, None]
    own_shift = block_shift[None, :]
    anchor_block = (first_block + own_local + own_shift) % block_count
    slot_index = shift_rank[None, :] - spare_count - (jnp.maximum(own_shift, 1) - 1) * CAP
    read_index = (
        (anchor_block // block_here * block_here + own_local) * block_here
        + anchor_block % block_here
    ) * CAP + slot_index
    read_index = jnp.where(own_shift == 0, 0, read_index)
    remote_rows = flat_incoming[read_index]
    local_rows = objective[own_local * NB + within_block[None, :]]
    pivoted = jnp.where((own_shift == 0)[..., None], local_rows, remote_rows).reshape(
        row_count, col_count
    )
    full_panel = lax.all_gather(panel, "col", axis=1, tiled=True)
    reduced = pivoted
    for panel_index in range(PANELS):
        owner_index = panel_index // block_here
        start_row = panel_index % block_here * NB
        diag_tile = full_panel[
            start_row : start_row + NB, panel_index * NB : (panel_index + 1) * NB
        ]
        safe_tile = jnp.where(my_index == owner_index, diag_tile, jnp.eye(NB, dtype=jnp.float32))
        solved = lax.linalg.triangular_solve(safe_tile, reduced, left_side=True, lower=True)
        solved = from_root(solved, "row", owner_index)
        update_term = jnp.dot(
            full_panel[:, panel_index * NB : (panel_index + 1) * NB],
            solved,
            precision=lax.Precision.HIGHEST,
            preferred_element_type=jnp.float32,
        )
        reduced = reduced - update_term
        replaced = jnp.where(my_index == owner_index, solved, reduced)
        reduced = replaced
    return reduced


def solution(mesh):
    in_specs = (P("row", "col"), P("row"), P("row", "col"))
    out_specs = P("row", "col")
    return jax.shard_map(body, mesh=mesh, in_specs=in_specs, out_specs=out_specs, check_vma=False)
```

profile of v0, /device:TPU:9, one launch (start us, length us, event | category | flops | bytes accessed | tf_op | source)
XLA Modules:
  0.0 357.0 jit_solution(368202324455760907)
XLA Ops:
  8.0 3.8 %sort.31 = (s32[512]{0:T(512)}, s32[512]{0:T(512)S(1)}) sort(s32[512]{0:T(512)S(1)} %get-tuple-element.43, s32[512]{0:T(512)S(1)} %iota.45), dimensions={0}, to_apply=%region_0.1 | sort | flops 4608 | bytes 8192 | tf_op jit(solution)/shard_map/jit(argsort)/sort | solution.py:28
  13.3 1.9 gather_fusion.2
  15.5 1.7 gather_fusion.3
  17.1 7.8 %all-to-all-start = ((f32[32,1,1,8,256]{4,3,2,1,0:T(8,128)}), f32[32,1,1,8,256]{4,3,2,1,0:T(8,128)S(1)}, u32[]{:S(2)}, u32[]{:S(2)}) async-start(f32[32,1,1,8,256]{4,3,2,1,0:T(8,128)} %bitcast.5), calls=%async_computation | async-start | bytes 524288 | tf_op jit(solution)/shard_map/all_to_all | solution.py:40
  25.1 3.8 %sort.32 = (s32[512]{0:T(512)}, s32[512]{0:T(512)S(1)}) sort(s32[512]{0:T(512)S(1)} %get-tuple-element.8, s32[512]{0:T(512)S(1)} %iota.47), dimensions={0}, to_apply=%region_1.2 | sort | flops 4608 | bytes 8192 | tf_op jit(solution)/shard_map/jit(argsort)/sort | solution.py:29
  28.9 1.6 gather_fusion
  30.5 2.4 all-to-all-done
  32.9 1.6 gather_fusion.4
  34.6 21.3 %all-gather.2.cloned.1.call-done = f32[512,1024]{1,0:T(8,128)} async-done(((f32[512,128]{1,0:T(8,128)}), f32[512,1024]{1,0:T(8,128)}) %all-gather.2.cloned.1.call-update) | async-done | bytes 2097168 | tf_op jit(solution)/shard_map/all_gather | solution.py:56
  55.9 2.8 fusion.4
  58.7 7.6 %while.4 = (s32[]{:T(128)}, f32[512,512]{1,0:T(8,128)S(1)}, s32[4,2]{0,1:T(2,128)S(1)}, f32[4,128,128]{2,1,0:T(8,128)S(1)}, s32[]{:T(128)}) while((s32[]{:T(128)}, f32[512,512]{1,0:T(8,128)S(1)}, s32[4,2]{0,1:T(2,128)S(1)}, f32[4,128,128]{2,1,0:T(8,128)S(1)}, s32[]{:T(128)}) %tuple.38), condition=%wide.while_cond, body=%wide.while_body.sunk | while | flops 2 | bytes 131181 | solution.py:65
  66.4 39.3 %custom-call.4 = f32[4,128,128]{1,2,0:T(8,128)S(1)} custom-call(f32[4,128,128]{2,1,0:T(8,128)S(1)} %get-tuple-element.24), custom_call_target="InvertDiagBlocksLowerTriangular" | custom-call | tf_op jit(solution)/shard_map/triangular_solve/custom-call.1 | solution.py:65
  107.2 1.5 convolution_subtract_fusion.2
  110.1 11.6 %while.5 = (s32[]{:T(128)}, f32[512,512]{1,0:T(8,128)}, s32[4,2]{0,1:T(2,128)S(1)}, f32[4,128,128]{2,1,0:T(8,128)S(1)}, s32[]{:T(128)}) while((s32[]{:T(128)}, f32[512,512]{1,0:T(8,128)}, s32[4,2]{0,1:T(2,128)S(1)}, f32[4,128,128]{2,1,0:T(8,128)S(1)}, s32[]{:T(128)}) %tuple.50), condition=%wide.while_cond.clone, body=%wide.while_body.clone.sunk | while | flops 2 | bytes 131181 | solution.py:65
  110.8 2.2 bitcast_dynamic-update-slice_fusion.5
  113.7 2.2 bitcast_dynamic-update-slice_fusion.5
  116.6 2.2 bitcast_dynamic-update-slice_fusion.5
  119.5 2.2 bitcast_dynamic-update-slice_fusion.5
  122.4 40.1 %custom-call.5 = f32[4,128,128]{1,2,0:T(8,128)S(1)} custom-call(f32[4,128,128]{2,1,0:T(8,128)} %copy-done.5), custom_call_target="InvertDiagBlocksLowerTriangular" | custom-call | tf_op jit(solution)/shard_map/triangular_solve/custom-call.1 | solution.py:65
  162.6 63.6 %all-reduce.3.cloned.1.call-done = f32[512,256]{1,0:T(8,128)} async-done(((f32[512,256]{1,0:T(8,128)}), f32[512,256]{1,0:T(8,128)}) %all-reduce.3.cloned.1.call-update) | async-done | bytes 524304 | tf_op jit(solution)/shard_map/psum | solution.py:14
  226.2 2.2 fusion.3
  231.7 1.3 convolution_subtract_fusion
  234.2 113.3 %all-reduce.5.cloned.1.call-done = f32[512,256]{1,0:T(8,128)} async-done(((f32[512,256]{1,0:T(8,128)}), f32[512,256]{1,0:T(8,128)}) %all-reduce.5.cloned.1.call-update) | async-done | bytes 524304 | tf_op jit(solution)/shard_map/psum | solution.py:14
  347.5 3.0 fusion.1
  (76 shorter events, 21.5 us)
Async XLA Ops:
  6.5 8.9 %copy-start = (f32[512,256]{1,0:T(8,128)S(1)}, f32[512,256]{1,0:T(8,128)}, u32[]{:S(2)}) copy-start(f32[512,256]{1,0:T(8,128)} %param.5) | copy-start | bytes 1572868
  6.5 49.4 %all-gather.2.cloned.1.call-start = ((), (), s32[]{:S(2)}) async-start(), calls=%async_computation.1 | async-start | bytes 2359296 | tf_op jit(solution)/shard_map/all_gather | solution.py:56
  17.1 15.7 %all-to-all-start = ((f32[32,1,1,8,256]{4,3,2,1,0:T(8,128)}), f32[32,1,1,8,256]{4,3,2,1,0:T(8,128)S(1)}, u32[]{:S(2)}, u32[]{:S(2)}) async-start(f32[32,1,1,8,256]{4,3,2,1,0:T(8,128)} %bitcast.5), calls=%async_computation | async-start | bytes 524288 | tf_op jit(solution)/shard_map/all_to_all | solution.py:40
  25.0 201.2 %all-reduce.3.cloned.1.call-start = ((), (), s32[]{:S(2)}) async-start(), calls=%async_computation.2 | async-start | bytes 1048576 | tf_op jit(solution)/shard_map/psum | solution.py:14
  66.4 40.2 %copy-start.4 = (f32[512,512]{1,0:T(8,128)}, f32[512,512]{1,0:T(8,128)S(1)}, u32[]{:S(2)}) copy-start(f32[512,512]{1,0:T(8,128)S(1)} %get-tuple-element.146) | copy-start | bytes 3145732
  106.9 119.3 %copy-start.1 = (f32[512,1024]{1,0:T(8,128)S(1)}, f32[512,1024]{1,0:T(8,128)}, u32[]{:S(2)}) copy-start(f32[512,1024]{1,0:T(8,128)} %all-gather.2.cloned.1.call-done) | copy-start | bytes 6291460
  109.9 237.6 %all-reduce.5.cloned.1.call-start = ((), (), s32[]{:S(2)}) async-start(), calls=%async_computation.3 | async-start | bytes 1048576 | tf_op jit(solution)/shard_map/psum | solution.py:14
  121.7 0.7 copy-start.5
  228.4 3.3 copy-start.2
  233.0 114.5 %copy-start.3 = (f32[512,256]{1,0:T(8,128)S(1)}, f32[512,256]{1,0:T(8,128)}, u32[]{:S(2)}) copy-start(f32[512,256]{1,0:T(8,128)} %copy-done.2) | copy-start | bytes 1572868
Sparse Core Ops, SparseCore 0:
  9.1 46.7 all-gather.1
  110.0 116.1 all-reduce.2
  234.3 113.1 all-reduce.4
where the time goes:
time: 359 us; the launch traced here: 357 us
  waiting for transfers between devices  201 us (56%)
  other arithmetic  93.1 us (26%)
  local copies, waits for them, and re-layouts  27.5 us (8%)
  between operations  13.5 us (4%)
  matrix products  13.3 us (4%)
  starting transfers between devices  8.11 us (2%)
    psum x2, waiting for transfers between devices, from_root(): return lax.psum(block, axis)  177 us
    another operation x4, other arithmetic, body(): lax.linalg.triangular_solve(safe_tile, reduced, left_side=True, lower=True)  82.3 us
    all_gather x1, waiting for transfers between devices, body(): full_panel = lax.all_gather(panel, 'col', axis=1, tiled=True)  21.3 us
    another operation x27, local copies, waits for them, and re-layouts, body(): lax.linalg.triangular_solve(safe_tile, reduced, left_side=True, lower=True)  19.1 us
    another operation x14, matrix products, body(): lax.linalg.triangular_solve(safe_tile, reduced, left_side=True, lower=True)  8.08 us
    all_to_all x1, starting transfers between devices, body(): lax.all_to_all(outgoing, 'row', split_axis=0, concat_axis=0, tiled=True)  7.85 us
  transfers between devices with their start and end apart: 4, of which 4 were waited for; matrix products, arithmetic and copies ran while one was open for 19% of the time, Pallas kernels for 0%

commit v1 on v0

v1 whole, which is shorter than its diff:
```python
import jax
import jax.numpy as jnp
from jax import lax
from jax.experimental import pallas as pl
from jax.experimental.pallas import tpu as pltpu
from jax.sharding import PartitionSpec as P

NB = 512
PIECE = 128
CAP = 8
ROWS = 32
CHIPS = 16
COLS = 8
HALF = NB // 2
PART = NB // ROWS
F32 = jnp.float32
BF16 = jnp.bfloat16
MESH = pl.DeviceIdType.MESH


def dot(a, b):
    return jnp.dot(a, b, precision=lax.Precision.HIGHEST, preferred_element_type=F32)


def pick(onehot, x):
    high = x.astype(BF16)
    rest = x - high.astype(F32)
    mid = rest.astype(BF16)
    low = (rest - mid.astype(F32)).astype(BF16)
    out = jnp.dot(onehot, high, preferred_element_type=F32)
    out = out + jnp.dot(onehot, mid, preferred_element_type=F32)
    return out + jnp.dot(onehot, low, preferred_element_type=F32)


def iota(shape, axis):
    return lax.broadcasted_iota(jnp.int32, shape, axis)


def triangle_inverse(tile):
    size = tile.shape[0]
    i, j = iota((size, size), 0), iota((size, size), 1)
    diag = jnp.where(i == j, tile, 0.0)
    down = 1.0 / jnp.sum(diag, axis=1, keepdims=True)
    across = 1.0 / jnp.sum(diag, axis=0, keepdims=True)
    below = jnp.where(i > j, tile, 0.0) * down
    inverse = jnp.where(i == j, 1.0, 0.0) - jnp.where((i >> 1) == (j >> 1), below, 0.0)
    block = 2
    level = 1
    while block < size:
        joined = ((i >> (level + 1)) == (j >> (level + 1))) & ((i >> level) != (j >> level))
        inverse = inverse - dot(dot(inverse, jnp.where(joined, below, 0.0)), inverse)
        block, level = 2 * block, level + 1
    return inverse * across


def kernel(
    obj_ref, piv_ref, panel_ref, out_ref,
    gathered, outgoing, incoming, solved, pivoted,
    row_send, row_recv, ring_send, ring_recv,
    part_send, part_recv, spread_send, spread_recv, pair_send, pair_recv, next_send, next_recv,
):
    r = lax.axis_index("row")
    z = lax.axis_index("col")
    right = {"col": lax.rem(z + 1, COLS)}
    left = {"col": lax.rem(z + COLS - 1, COLS)}

    barrier = pltpu.get_barrier_semaphore()

    def greet(step, _):
        peer = {"row": lax.rem(r + step, ROWS)}
        pl.semaphore_signal(barrier, inc=1, device_id=peer, device_id_type=MESH)
        return 0

    lax.fori_loop(1, ROWS, greet, 0)
    pl.semaphore_signal(barrier, inc=1, device_id=right, device_id_type=MESH)
    pl.semaphore_signal(barrier, inc=1, device_id=left, device_id_type=MESH)

    gathered[z] = panel_ref[...]
    for k in range(2):
        for b in range(4):
            @pl.when((r == k) & (z == 4 * k + b))
            def _():
                gathered[4 * k + b, b * PIECE : (b + 1) * PIECE] = triangle_inverse(
                    panel_ref[b * PIECE : (b + 1) * PIECE]
                )

    piv = piv_ref[...]
    target = piv & (NB - 1)
    shift = ((piv >> 9) - r) & (ROWS - 1)
    has = jnp.where(iota((ROWS, NB), 0) == shift, 1.0, 0.0)
    before = jnp.where(iota((NB, NB), 0) < iota((NB, NB), 1), 1.0, 0.0).astype(BF16)
    count = jnp.dot(has.astype(BF16), before, preferred_element_type=F32)
    rank = jnp.sum(has * count, axis=0, keepdims=True).astype(jnp.int32)
    slot = jnp.where(shift > 0, (shift - 1) * CAP + rank, -1)
    own = jnp.where(shift > 0, -1, target)
    slot_at = jnp.where(iota((HALF, NB), 0) == slot, 1.0, 0.0).astype(BF16)
    target_at = jnp.where(iota((NB, NB), 0) == target, 1.0, 0.0).astype(BF16)
    chosen = lax.dot_general(
        slot_at, target_at, (((1,), (1,)), ((), ())), preferred_element_type=F32
    ).astype(BF16)
    obj = obj_ref[...]
    outgoing[...] = pick(chosen, obj)
    incoming[(ROWS - 1) * CAP :] = jnp.zeros((CAP, incoming.shape[1]), F32)

    pl.semaphore_wait(barrier, ROWS + 1)

    def ring(direction, half, hop, shard):
        place = gathered.at[shard, pl.ds(half * HALF, HALF)]
        return pltpu.make_async_remote_copy(
            src_ref=place, dst_ref=place,
            send_sem=ring_send.at[direction, half, hop],
            recv_sem=ring_recv.at[direction, half, hop],
            device_id=right if direction == 0 else left, device_id_type=MESH,
        )

    def ring_start(direction, half, hop):
        shard = lax.rem(z - hop + COLS, COLS) if direction == 0 else lax.rem(z + hop, COLS)
        ring(direction, half, hop, shard).start()

    def ring_arrive(direction, half, hop):
        shard = (
            lax.rem(z - hop - 1 + COLS, COLS) if direction == 0 else lax.rem(z + hop + 1, COLS)
        )
        ring(direction, half, hop, shard).wait_recv()

    def ring_sent(direction, half, hop):
        ring(direction, half, hop, z).wait_send()

    for half in (0, 1):
        for direction in (0, 1):
            ring_start(direction, half ^ direction, 0)

    def pass_row(step, _):
        place = pl.ds(pl.multiple_of((step - 1) * CAP, CAP), CAP)
        pltpu.make_async_remote_copy(
            src_ref=outgoing.at[place], dst_ref=incoming.at[place],
            send_sem=row_send, recv_sem=row_recv,
            device_id={"row": lax.rem(r - step + ROWS, ROWS)}, device_id_type=MESH,
        ).start()
        return 0

    lax.fori_loop(1, ROWS, pass_row, 0)

    both = jnp.concatenate([slot, own, slot, own, slot, own, slot, own], axis=0).astype(F32)
    turned = both.T.astype(jnp.int32)
    own_at = jnp.where(iota((NB, NB), 1) == turned[:, 1:2], 1.0, 0.0).astype(BF16)
    pivoted[...] = pick(own_at, obj)

    all_rows = pl.ds(0, (ROWS - 1) * CAP)
    rows_done = pltpu.make_async_remote_copy(
        src_ref=outgoing.at[all_rows], dst_ref=incoming.at[all_rows],
        send_sem=row_send, recv_sem=row_recv, device_id=right, device_id_type=MESH,
    )
    rows_done.wait_recv()
    from_slot = jnp.where(iota((NB, HALF), 1) == turned[:, 0:1], 1.0, 0.0).astype(BF16)
    pivoted[...] = pivoted[...] + pick(from_slot, incoming[...])

    for hop in range(4):
        for half in (0, 1):
            for direction in (0, 1):
                h = half ^ direction
                if half == 0 or hop < 3:
                    ring_arrive(direction, h, hop)
                    if hop + 1 < (4 if half == 0 else 3):
                        ring_start(direction, h, hop + 1)

    def solve(k):
        for b in range(4):
            at = slice(b * PIECE, (b + 1) * PIECE)
            x = dot(gathered[4 * k + b, at], pivoted[at])
            solved[k, at] = x
            if b < 3:
                rest = slice((b + 1) * PIECE, NB)
                pivoted[rest] = pivoted[rest] - dot(gathered[4 * k + b, rest], x)

    def part_copy(k, part, send, recv, device):
        place = solved.at[k, pl.ds(pl.multiple_of(part * PART, PART), PART)]
        return pltpu.make_async_remote_copy(
            src_ref=place, dst_ref=place, send_sem=send.at[k], recv_sem=recv.at[k],
            device_id={"row": device}, device_id_type=MESH,
        )

    def rows_of(k, start, count, send, recv, device=None):
        place = solved.at[k, pl.ds(start, count)]
        return pltpu.make_async_remote_copy(
            src_ref=place, dst_ref=place, send_sem=send, recv_sem=recv,
            device_id=right if device is None else {"row": device}, device_id_type=MESH,
        )

    core = lax.rem(r, 2)
    chip = r // 2

    def scatter(k):
        def one(device, _):
            c, i = lax.rem(device, 2), device // 2
            part_copy(k, c * CHIPS + i, part_send, part_recv, device).start()
            return 0

        lax.fori_loop(2, ROWS, one, 0)

        def first(device, _):
            part_copy(k, lax.rem(device, 2) * CHIPS, spread_send, spread_recv, device).start()
            return 0

        lax.fori_loop(2, ROWS, first, 0)

    def scatter_sent(k):
        rows_of(k, 0, 30 * PART, part_send.at[k], part_recv.at[k]).wait_send()
        rows_of(k, 0, 30 * PART, spread_send.at[k], spread_recv.at[k]).wait_send()

    def spread(k):
        part_copy(k, 0, part_send, part_recv, r).wait_recv()

        def one(step, _):
            other = lax.rem(chip - 1 + step, CHIPS - 1) + 1
            part_copy(k, core * CHIPS + chip, spread_send, spread_recv, other * 2 + core).start()
            return 0

        lax.fori_loop(1, CHIPS - 1, one, 0)

    def pair(k):
        rows_of(k, 0, 15 * PART, spread_send.at[k], spread_recv.at[k]).wait_recv()
        start = pl.multiple_of(core * HALF, HALF)
        rows_of(k, start, HALF, pair_send.at[k], pair_recv.at[k], r + 1 - 2 * core).start()

    def pair_done(k):
        rows_of(k, 0, HALF, pair_send.at[k], pair_recv.at[k]).wait_recv()

    def update(k):
        full = jnp.concatenate([gathered[4 * k + b] for b in range(4)], axis=1)
        return dot(full, solved[k])

    @pl.when(r == 0)
    def _():
        solve(0)
        whole = rows_of(0, 0, NB, next_send, next_recv, 1)
        whole.start()
        scatter(0)
        out_ref[...] = solved[0]
        whole.wait_send()
        scatter_sent(0)

    @pl.when(r == 1)
    def _():
        rows_of(0, 0, NB, next_send, next_recv, 0).wait_recv()
        pivoted[...] = pivoted[...] - update(0)
        solve(1)
        scatter(1)
        out_ref[...] = solved[1]
        scatter_sent(1)

    @pl.when(r >= 2)
    def _():
        for k in range(2):
            spread(k)
            pair(k)
            pair_done(k)
            out_ref[...] = (pivoted[...] if k == 0 else out_ref[...]) - update(k)
        for k in range(2):
            rows_of(k, 0, 14 * PART, spread_send.at[k], spread_recv.at[k]).wait_send()
            rows_of(k, 0, HALF, pair_send.at[k], pair_recv.at[k]).wait_send()

    rows_done.wait_send()
    for hop in range(4):
        for half in (0, 1):
            for direction in (0, 1):
                if half == 0 or hop < 3:
                    ring_sent(direction, half ^ direction, hop)


def body(objective, pivots, panel):
    width = objective.shape[1]
    dma = pltpu.SemaphoreType.DMA
    vmem = pl.BlockSpec(memory_space=pltpu.VMEM)
    return pl.pallas_call(
        kernel,
        out_shape=jax.ShapeDtypeStruct(objective.shape, F32),
        in_specs=[vmem] * 3,
        out_specs=vmem,
        scratch_shapes=[
            pltpu.VMEM((COLS, NB, PIECE), F32),
            pltpu.VMEM((HALF, width), F32),
            pltpu.VMEM((HALF, width), F32),
            pltpu.VMEM((2, NB, width), F32),
            pltpu.VMEM((NB, width), F32),
            dma, dma,
            dma((2, 2, 4)), dma((2, 2, 4)),
            dma((2,)), dma((2,)), dma((2,)), dma((2,)), dma((2,)), dma((2,)), dma, dma,
        ],
        compiler_params=pltpu.CompilerParams(
            collective_id=0, has_side_effects=True, vmem_limit_bytes=48 * 1024 * 1024
        ),
        name="zonal",
    )(objective, pivots.reshape(1, NB), panel)


def solution(mesh):
    in_specs = (P("row", "col"), P("row"), P("row", "col"))
    out_specs = P("row", "col")
    return jax.shard_map(body, mesh=mesh, in_specs=in_specs, out_specs=out_specs, check_vma=False)
```

time: 359 us -> 62.4 us (0.17)
  waiting for transfers between devices: 201 us -> 0 us
  other arithmetic: 93.1 us -> 0 us
  Pallas kernels: 0 us -> 58.7 us
  local copies, waits for them, and re-layouts: 27.5 us -> 3.47 us
  between operations: 13.5 us -> 0.01 us
  matrix products: 13.3 us -> 0 us
  starting transfers between devices: 8.11 us -> 0 us
    psum x2 -> x0, waiting for transfers between devices: 177 us -> none  [from_root(): return lax.psum(block, axis)]
    another operation x4 -> x0, other arithmetic: 82.3 us -> none  [body(): lax.linalg.triangular_solve(safe_tile, reduced, left_side=True, lower=True)]
    pallas_call x0 -> x1, Pallas kernels: none -> 58.7 us  [body(): pl.pallas_call(kernel, out_shape=jax.ShapeDtypeStruct(objective.shape, F3...]
    all_gather x1 -> x0, waiting for transfers between devices: 21.3 us -> none  [body(): full_panel = lax.all_gather(panel, 'col', axis=1, tiled=True)]
    another operation x27 -> x0, local copies, waits for them, and re-layouts: 19.1 us -> none  [body(): lax.linalg.triangular_solve(safe_tile, reduced, left_side=True, lower=True)]
    another operation x14 -> x0, matrix products: 8.08 us -> none  [body(): lax.linalg.triangular_solve(safe_tile, reduced, left_side=True, lower=True)]
    all_to_all x1 -> x0, starting transfers between devices: 7.85 us -> none  [body(): lax.all_to_all(outgoing, 'row', split_axis=0, concat_axis=0, tiled=True)]
    sort x2 -> x0, other arithmetic: 7.55 us -> none  [the longest x1 3.78 us: body(): shift_rank = jnp.argsort(shift_order, stable=True)]
  transfers between devices with their start and end apart: 4 -> 0, of which waited for: 4 -> 0; matrix products, arithmetic and copies ran while one was open for 19% -> 0% of each run, Pallas kernels for 0% -> 0%
where the time goes in v1:
time: 62.4 us; the launch traced here: 62.2 us
  Pallas kernels  58.7 us (94%)
  local copies, waits for them, and re-layouts  3.47 us (6%)
    pallas_call x1, Pallas kernels, body(): pl.pallas_call(kernel, out_shape=jax.ShapeDtypeStruct(objective.shape, F3...  58.7 us
    unnamed x7, local copies, waits for them, and re-layouts  3.47 us

profile of v1, /device:TPU:9, one launch (start us, length us, event | category | flops | bytes accessed | tf_op | source)
XLA Modules:
  0.0 62.2 jit_solution(15429795015195120281)
XLA Ops:
  0.0 0.0 copy-start
  0.0 1.0 %copy-done = f32[512,256]{1,0:T(8,128)S(1)} copy-done((f32[512,256]{1,0:T(8,128)S(1)}, f32[512,256]{1,0:T(8,128)}, u32[]{:S(2)}) %copy-start) | copy-done | bytes 524312
  1.0 0.0 copy-start.1
  1.0 0.9 %copy-done.1 = f32[512,128]{1,0:T(8,128)S(1)} copy-done((f32[512,128]{1,0:T(8,128)S(1)}, f32[512,128]{1,0:T(8,128)}, u32[]{:S(2)}) %copy-start.1) | copy-done | bytes 262168
  2.0 0.0 copy-start.2
  2.0 0.7 %copy-done.2 = s32[512]{0:T(512)S(1)} copy-done((s32[512]{0:T(512)S(1)}, s32[512]{0:T(512)}, u32[]{:S(2)}) %copy-start.2) | copy-done | bytes 2072
  2.7 58.7 %zonal.1 = f32[512,256]{1,0:T(8,128)S(1)} custom-call(f32[512,256]{1,0:T(8,128)S(1)} %copy-done, s32[1,512]{1,0:T(1,128)S(1)} %bitcast.1, f32[512,128]{1,0:T(8,128)S(1)} %copy-done.1), custom_call_target="tpu_custom_call" | custom-call | tf_op jit(solution)/shard_map/zonal/pallas_call | solution.py:275
  61.4 0.8 %copy.5 = f32[512,256]{1,0:T(8,128)} copy(f32[512,256]{1,0:T(8,128)S(1)} %zonal.1) | data formatting | bytes 1048576
Async XLA Ops:
  0.0 1.0 %copy-start = (f32[512,256]{1,0:T(8,128)S(1)}, f32[512,256]{1,0:T(8,128)}, u32[]{:S(2)}) copy-start(f32[512,256]{1,0:T(8,128)} %obj_ref.1) | copy-start | bytes 1572868
  1.0 0.9 %copy-start.1 = (f32[512,128]{1,0:T(8,128)S(1)}, f32[512,128]{1,0:T(8,128)}, u32[]{:S(2)}) copy-start(f32[512,128]{1,0:T(8,128)} %panel_ref.1) | copy-start | bytes 786436
  2.0 0.7 %copy-start.2 = (s32[512]{0:T(512)S(1)}, s32[512]{0:T(512)}, u32[]{:S(2)}) copy-start(s32[512]{0:T(512)} %param.4) | copy-start | bytes 6148

commit v2 on v1

v2 whole, which is shorter than its diff:
```python
import jax
import jax.numpy as jnp
from jax import lax
from jax.experimental import pallas as pl
from jax.experimental.pallas import tpu as pltpu
from jax.sharding import PartitionSpec as P

NB = 512
PIECE = 128
CAP = 8
ROWS = 32
CHIPS = 16
COLS = 8
HALF = NB // 2
PART = HALF // CHIPS
HELPER = 4
F32 = jnp.float32
BF16 = jnp.bfloat16
MESH = pl.DeviceIdType.MESH


def dot(a, b):
    return jnp.dot(a, b, precision=lax.Precision.HIGHEST, preferred_element_type=F32)


def pick(onehot, x):
    high = x.astype(BF16)
    rest = x - high.astype(F32)
    mid = rest.astype(BF16)
    low = (rest - mid.astype(F32)).astype(BF16)
    out = jnp.dot(onehot, high, preferred_element_type=F32)
    out = out + jnp.dot(onehot, mid, preferred_element_type=F32)
    return out + jnp.dot(onehot, low, preferred_element_type=F32)


def iota(shape, axis):
    return lax.broadcasted_iota(jnp.int32, shape, axis)


def triangle_inverse(tile):
    size = tile.shape[0]
    i, j = iota((size, size), 0), iota((size, size), 1)
    diag = jnp.where(i == j, tile, 0.0)
    down = 1.0 / jnp.sum(diag, axis=1, keepdims=True)
    across = 1.0 / jnp.sum(diag, axis=0, keepdims=True)
    below = jnp.where(i > j, tile, 0.0) * down
    inverse = jnp.where(i == j, 1.0, 0.0) - jnp.where((i >> 1) == (j >> 1), below, 0.0)
    block = 2
    level = 1
    while block < size:
        joined = ((i >> (level + 1)) == (j >> (level + 1))) & ((i >> level) != (j >> level))
        inverse = inverse - dot(dot(inverse, jnp.where(joined, below, 0.0)), inverse)
        block, level = 2 * block, level + 1
    return inverse * across


def kernel(
    obj_hbm, piv_hbm, panel_hbm, out_ref,
    obj_ref, piv_ref, obj_sem, piv_sem, panel_sem,
    gathered, outgoing, incoming, solved, pivoted,
    row_send, row_recv, ring_send, ring_recv,
    part_send, part_recv, spread_send, spread_recv, pair_send, pair_recv, next_send, next_recv,
):
    r = lax.axis_index("row")
    z = lax.axis_index("col")
    right = {"col": lax.rem(z + 1, COLS)}
    left = {"col": lax.rem(z + COLS - 1, COLS)}

    panel_in = pltpu.make_async_copy(panel_hbm, gathered.at[z], panel_sem)
    obj_in = pltpu.make_async_copy(obj_hbm, obj_ref, obj_sem)
    piv_in = pltpu.make_async_copy(piv_hbm, piv_ref, piv_sem)
    panel_in.start()
    piv_in.start()
    obj_in.start()

    barrier = pltpu.get_barrier_semaphore()

    def greet(step, _):
        peer = {"row": lax.rem(r + step, ROWS)}
        pl.semaphore_signal(barrier, inc=1, device_id=peer, device_id_type=MESH)
        return 0

    lax.fori_loop(1, ROWS, greet, 0)
    pl.semaphore_signal(barrier, inc=1, device_id=right, device_id_type=MESH)
    pl.semaphore_signal(barrier, inc=1, device_id=left, device_id_type=MESH)

    @pl.when((r < 2) & (z // 4 == r))
    def _():
        panel_in.wait()
        place = pl.ds(pl.multiple_of(lax.rem(z, 4) * PIECE, PIECE), PIECE)
        gathered[z, place] = triangle_inverse(gathered[z, place])

    @pl.when(jnp.logical_not((r < 2) & (z // 4 == r)))
    def _():
        panel_in.wait()

    piv_in.wait()
    piv = piv_ref[...]
    target = piv & (NB - 1)
    shift = ((piv >> 9) - r) & (ROWS - 1)
    has = jnp.where(iota((ROWS, NB), 0) == shift, 1.0, 0.0)
    before = jnp.where(iota((NB, NB), 0) < iota((NB, NB), 1), 1.0, 0.0).astype(BF16)
    count = jnp.dot(has.astype(BF16), before, preferred_element_type=F32)
    rank = jnp.sum(has * count, axis=0, keepdims=True).astype(jnp.int32)
    slot = jnp.where(shift > 0, (shift - 1) * CAP + rank, -1)
    own = jnp.where(shift > 0, -1, target)
    slot_at = jnp.where(iota((HALF, NB), 0) == slot, 1.0, 0.0).astype(BF16)
    target_at = jnp.where(iota((NB, NB), 0) == target, 1.0, 0.0).astype(BF16)
    chosen = lax.dot_general(
        slot_at, target_at, (((1,), (1,)), ((), ())), preferred_element_type=F32
    ).astype(BF16)
    obj_in.wait()
    obj = obj_ref[...]
    outgoing[...] = pick(chosen, obj)
    incoming[(ROWS - 1) * CAP :] = jnp.zeros((CAP, incoming.shape[1]), F32)

    pl.semaphore_wait(barrier, ROWS + 1)

    def first_step(shard):
        return jnp.where(r >= 2, 0, jnp.where(r == 0, shard, jnp.maximum(shard - 4, 0)))

    def ring(direction, quarter, hop, shard):
        place = gathered.at[shard, pl.ds(quarter * PIECE, PIECE)]
        return pltpu.make_async_remote_copy(
            src_ref=place, dst_ref=place,
            send_sem=ring_send.at[direction, quarter, hop],
            recv_sem=ring_recv.at[direction, quarter, hop],
            device_id=right if direction == 0 else left, device_id_type=MESH,
        )

    def shard_of(direction, hop):
        return lax.rem(z - hop + COLS, COLS) if direction == 0 else lax.rem(z + hop, COLS)

    def hops(direction, quarter):
        return 4 if (quarter < 2) == (direction == 0) else 3

    def ring_start(direction, quarter, hop):
        shard = shard_of(direction, hop)

        @pl.when(quarter >= first_step(shard))
        def _():
            ring(direction, quarter, hop, shard).start()

    def ring_step(direction, quarter, hop):
        shard = shard_of(direction, hop + 1)

        @pl.when(quarter >= first_step(shard))
        def _():
            ring(direction, quarter, hop, shard).wait_recv()
            if hop + 1 < hops(direction, quarter):
                ring(direction, quarter, hop + 1, shard).start()

    def ring_sent(direction, quarter, hop):
        shard = shard_of(direction, hop)

        @pl.when(quarter >= first_step(shard))
        def _():
            ring(direction, quarter, hop, shard).wait_send()

    ORDER = [(0, 0), (1, 2), (0, 1), (1, 3), (0, 2), (1, 0), (0, 3), (1, 1)]

    def ring_hop(hop, part):
        for direction, quarter in ORDER[4 * part : 4 * part + 4]:
            if hop < hops(direction, quarter):
                ring_step(direction, quarter, hop)

    for direction, quarter in ORDER:
        ring_start(direction, quarter, 0)

    def pass_row(step, _):
        place = pl.ds(pl.multiple_of((step - 1) * CAP, CAP), CAP)
        pltpu.make_async_remote_copy(
            src_ref=outgoing.at[place], dst_ref=incoming.at[place],
            send_sem=row_send, recv_sem=row_recv,
            device_id={"row": lax.rem(r - step + ROWS, ROWS)}, device_id_type=MESH,
        ).start()
        return 0

    lax.fori_loop(1, ROWS, pass_row, 0)

    both = jnp.concatenate([slot, own, slot, own, slot, own, slot, own], axis=0).astype(F32)
    turned = both.T.astype(jnp.int32)
    own_at = jnp.where(iota((NB, NB), 1) == turned[:, 1:2], 1.0, 0.0).astype(BF16)
    pivoted[...] = pick(own_at, obj)

    all_rows = pl.ds(0, (ROWS - 1) * CAP)
    rows_done = pltpu.make_async_remote_copy(
        src_ref=outgoing.at[all_rows], dst_ref=incoming.at[all_rows],
        send_sem=row_send, recv_sem=row_recv, device_id=right, device_id_type=MESH,
    )
    from_slot = jnp.where(iota((NB, HALF), 1) == turned[:, 0:1], 1.0, 0.0).astype(BF16)

    def take_rows():
        rows_done.wait_recv()
        pivoted[...] = pivoted[...] + pick(from_slot, incoming[...])

    core = lax.rem(r, 2)
    chip = r // 2

    def part_copy(group, part, half, send, recv, device):
        place = solved.at[
            pl.ds(pl.multiple_of(group * HALF + part * PART, PART), PART),
            pl.ds(pl.multiple_of(half * PIECE, PIECE), PIECE),
        ]
        return pltpu.make_async_remote_copy(
            src_ref=place, dst_ref=place, send_sem=send.at[group], recv_sem=recv.at[group],
            device_id={"row": device}, device_id_type=MESH,
        )

    def parts(group, count, send, recv):
        place = solved.at[pl.ds(0, count * PART), pl.ds(0, PIECE)]
        return pltpu.make_async_remote_copy(
            src_ref=place, dst_ref=place, send_sem=send.at[group], recv_sem=recv.at[group],
            device_id=right, device_id_type=MESH,
        )

    def block_copy(block):
        place = solved.at[pl.ds(block * PIECE, PIECE)]
        return pltpu.make_async_remote_copy(
            src_ref=place, dst_ref=place,
            send_sem=next_send.at[block], recv_sem=next_recv.at[block],
            device_id={"row": lax.rem(r + 1, ROWS)}, device_id_type=MESH,
        )

    def scatter(group):
        def one(device, _):
            part_copy(
                group, device // 2, lax.rem(device, 2), part_send, part_recv, device
            ).start()
            return 0

        lax.fori_loop(2, ROWS, one, 0)
        for half in range(2):
            part_copy(group, 0, half, part_send, part_recv, 2 * HELPER + half).start()

    def solve(k):
        for b in range(4):
            at = slice(b * PIECE, (b + 1) * PIECE)
            x = dot(gathered[4 * k + b, at], pivoted[at])
            solved[k * NB + b * PIECE : k * NB + (b + 1) * PIECE] = x
            if k == 0:
                block_copy(b).start()
            if b % 2 == 1:
                scatter(2 * k + b // 2)
            if b < 3:
                rest = slice((b + 1) * PIECE, NB)
                pivoted[rest] = pivoted[rest] - dot(gathered[4 * k + b, rest], x)
        out_ref[...] = solved[k * NB : (k + 1) * NB]
        for b in range(4):
            if k == 0:
                block_copy(b).wait_send()
        for half in range(2):
            place = solved.at[pl.ds(0, HALF)]
            pltpu.make_async_remote_copy(
                src_ref=place, dst_ref=place, send_sem=part_send.at[2 * k + half],
                recv_sem=part_recv.at[0], device_id=right, device_id_type=MESH,
            ).wait_send()

    def spread(group):
        def pass_on(part):
            def one(step, _):
                other = lax.rem(chip - 1 + step, CHIPS - 1) + 1
                part_copy(
                    group, part, core, spread_send, spread_recv, other * 2 + core
                ).start()
                return 0

            lax.fori_loop(1, CHIPS - 1, one, 0)

        @pl.when(chip == HELPER)
        def _():
            parts(group, 2, part_send, part_recv).wait_recv()
            pass_on(0)

        @pl.when(chip != HELPER)
        def _():
            parts(group, 1, part_send, part_recv).wait_recv()

        pass_on(chip)

    def pair_copy(group):
        place = solved.at[
            pl.ds(pl.multiple_of(group * HALF, HALF), HALF),
            pl.ds(pl.multiple_of(core * PIECE, PIECE), PIECE),
        ]
        return pltpu.make_async_remote_copy(
            src_ref=place, dst_ref=place,
            send_sem=pair_send.at[group], recv_sem=pair_recv.at[group],
            device_id={"row": r + 1 - 2 * core}, device_id_type=MESH,
        )

    def pair(group):
        @pl.when(chip == HELPER)
        def _():
            parts(group, 14, spread_send, spread_recv).wait_recv()

        @pl.when(chip != HELPER)
        def _():
            parts(group, 15, spread_send, spread_recv).wait_recv()

        pair_copy(group).start()

    def passed(group):
        @pl.when(chip == HELPER)
        def _():
            parts(group, 28, spread_send, spread_recv).wait_send()

        @pl.when(chip != HELPER)
        def _():
            parts(group, 14, spread_send, spread_recv).wait_send()

        pair_copy(group).wait_send()

    def update(group):
        left_part = jnp.concatenate([gathered[2 * group], gathered[2 * group + 1]], axis=1)
        rows = pl.ds(pl.multiple_of(group * HALF, HALF), HALF)
        pivoted[...] = pivoted[...] - dot(left_part, solved[rows])

    @pl.when(r == 0)
    def _():
        for hop in range(4):
            ring_hop(hop, 0)
            ring_hop(hop, 1)
            if hop == 1:
                take_rows()
        solve(0)

    @pl.when(r == 1)
    def _():
        for hop in range(4):
            ring_hop(hop, 0)
            ring_hop(hop, 1)
            if hop == 1:
                take_rows()
        for b in range(4):
            block_copy(b).wait_recv()
            pivoted[...] = pivoted[...] - dot(
                gathered[b], solved[b * PIECE : (b + 1) * PIECE]
            )
        solve(1)

    @pl.when(r >= 2)
    def _():
        last = lax.rem(z + COLS // 2, COLS) // 2
        ring_hop(0, 0)
        ring_hop(0, 1)
        take_rows()
        ring_hop(1, 0)
        spread(0)
        ring_hop(1, 1)
        spread(1)
        pair(0)
        ring_hop(2, 0)
        pair(1)
        spread(2)
        ring_hop(2, 1)
        spread(3)
        pair(2)
        ring_hop(3, 0)
        ring_hop(3, 1)
        pair(3)

        def early(group, _):
            pair_copy(group).wait_recv()

            @pl.when(group != last)
            def _():
                update(group)

            return 0

        lax.fori_loop(0, 3, early, 0)

        @pl.when(last != 3)
        def _():
            update(last)

        pair_copy(3).wait_recv()
        update(3)
        out_ref[...] = pivoted[...]
        for group in range(4):
            passed(group)

    rows_done.wait_send()
    for hop in range(4):
        for direction, quarter in ORDER:
            if hop < hops(direction, quarter):
                ring_sent(direction, quarter, hop)


def body(objective, pivots, panel):
    width = objective.shape[1]
    dma = pltpu.SemaphoreType.DMA
    vmem = pl.BlockSpec(memory_space=pltpu.VMEM)
    return pl.pallas_call(
        kernel,
        out_shape=jax.ShapeDtypeStruct(objective.shape, F32),
        in_specs=[pl.BlockSpec(memory_space=pl.ANY)] * 3,
        out_specs=vmem,
        scratch_shapes=[
            pltpu.VMEM(objective.shape, F32), pltpu.VMEM((1, NB), jnp.int32), dma, dma, dma,
            pltpu.VMEM((COLS, NB, PIECE), F32),
            pltpu.VMEM((HALF, width), F32),
            pltpu.VMEM((HALF, width), F32),
            pltpu.VMEM((2 * NB, width), F32),
            pltpu.VMEM((NB, width), F32),
            dma, dma,
            dma((2, 4, 4)), dma((2, 4, 4)),
            dma((4,)), dma((4,)), dma((4,)), dma((4,)), dma((4,)), dma((4,)), dma((4,)), dma((4,)),
        ],
        compiler_params=pltpu.CompilerParams(
            collective_id=0, has_side_effects=True, vmem_limit_bytes=60 * 1024 * 1024
        ),
        name="zonal",
    )(objective, pivots.reshape(1, NB), panel)


def solution(mesh):
    in_specs = (P("row", "col"), P("row"), P("row", "col"))
    out_specs = P("row", "col")
    return jax.shard_map(body, mesh=mesh, in_specs=in_specs, out_specs=out_specs, check_vma=False)
```

time: 62.4 us -> 48.5 us (0.78)
  the two profiles are of different devices: /device:TPU:9 before, /device:TPU:196 now
where the time goes in v2:
time: 48.5 us; the launch traced here: 48.3 us
  Pallas kernels  46.4 us (96%)
  local copies, waits for them, and re-layouts  1.87 us (4%)
    pallas_call x1, Pallas kernels, body(): pl.pallas_call(kernel, out_shape=jax.ShapeDtypeStruct(objective.shape, F3...  46.4 us
    unnamed x1, local copies, waits for them, and re-layouts  1.87 us

profile of v2, /device:TPU:196, one launch (start us, length us, event | category | flops | bytes accessed | tf_op | source)
XLA Modules:
  0.0 48.3 jit_solution(209772896358961984)
XLA Ops:
  0.0 46.4 %zonal.1 = f32[512,256]{1,0:T(8,128)} custom-call(f32[512,256]{1,0:T(8,128)} %obj_hbm.1, s32[1,512]{1,0:T(1,128)} %bitcast.1, f32[512,128]{1,0:T(8,128)} %panel_hbm.1), custom_call_target="tpu_custom_call" | custom-call | tf_op jit(solution)/shard_map/zonal/pallas_call | solution.py:395
  46.5 1.9 %copy.5 = f32[512,256]{1,0:T(8,128)} copy(f32[512,256]{1,0:T(8,128)} %zonal.1) | data formatting | bytes 1048576

commit v3 on v2

--- a/solution.py
+++ b/solution.py
@@ -392,6 +392,10 @@
     width = objective.shape[1]
     dma = pltpu.SemaphoreType.DMA
     vmem = pl.BlockSpec(memory_space=pltpu.VMEM)
+    arrays = [
+        pltpu.with_memory_space_constraint(array, pltpu.HBM)
+        for array in (objective, pivots.reshape(1, NB), panel)
+    ]
     return pl.pallas_call(
         kernel,
         out_shape=jax.ShapeDtypeStruct(objective.shape, F32),
@@ -409,10 +413,10 @@
             dma((4,)), dma((4,)), dma((4,)), dma((4,)), dma((4,)), dma((4,)), dma((4,)), dma((4,)),
         ],
         compiler_params=pltpu.CompilerParams(
-            collective_id=0, has_side_effects=True, vmem_limit_bytes=60 * 1024 * 1024
+            collective_id=0, has_side_effects=True, vmem_limit_bytes=48 * 1024 * 1024
         ),
         name="zonal",
-    )(objective, pivots.reshape(1, NB), panel)
+    )(*arrays)
 
 
 def solution(mesh):

time: 48.5 us -> 46.5 us (0.959)
  local copies, waits for them, and re-layouts: 1.87 us -> 0.8 us
  Pallas kernels: 46.4 us -> 45.6 us
    unnamed x1, local copies, waits for them, and re-layouts: 1.87 us -> 0.8 us
    pallas_call x1, Pallas kernels: 46.4 us -> 45.6 us  [body(): pl.pallas_call(kernel, out_shape=jax.ShapeDtypeStruct(objective.shape, F3...]
where the time goes in v3:
time: 46.5 us
  Pallas kernels  45.6 us (98%)
  local copies, waits for them, and re-layouts  0.8 us (2%)
    pallas_call x1, Pallas kernels, body(): pl.pallas_call(kernel, out_shape=jax.ShapeDtypeStruct(objective.shape, F3...  45.6 us

profile of v3, /device:TPU:196, one launch (start us, length us, event | category | flops | bytes accessed | tf_op | source)
XLA Modules:
  0.0 46.5 jit_solution(14428984899925334307)
XLA Ops:
  0.0 45.6 %zonal.1 = f32[512,256]{1,0:T(8,128)S(1)} custom-call(f32[512,256]{1,0:T(8,128)} %obj_hbm.1, s32[1,512]{1,0:T(1,128)} %bitcast.1, f32[512,128]{1,0:T(8,128)} %panel_hbm.1), custom_call_target="tpu_custom_call" | custom-call | tf_op jit(solution)/shard_map/zonal/pallas_call | solution.py:399
  45.7 0.8 %copy.5 = f32[512,256]{1,0:T(8,128)} copy(f32[512,256]{1,0:T(8,128)S(1)} %zonal.1) | data formatting | bytes 1048576

commit v4 on v3

--- a/solution.py
+++ b/solution.py
@@ -21,6 +21,18 @@
 
 def dot(a, b):
     return jnp.dot(a, b, precision=lax.Precision.HIGHEST, preferred_element_type=F32)
+
+
+def halves(x):
+    high = x.astype(BF16)
+    return high, (x - high.astype(F32)).astype(BF16)
+
+
+def dot3(a, b):
+    (a_high, a_low), (b_high, b_low) = halves(a), halves(b)
+    small = jnp.dot(a_high, b_low, preferred_element_type=F32)
+    small = small + jnp.dot(a_low, b_high, preferred_element_type=F32)
+    return small + jnp.dot(a_high, b_high, preferred_element_type=F32)
 
 
 def pick(onehot, x):
@@ -56,7 +68,7 @@
 
 def kernel(
     obj_hbm, piv_hbm, panel_hbm, out_ref,
-    obj_ref, piv_ref, obj_sem, piv_sem, panel_sem,
+    obj_ref, piv_ref, obj_sem, piv_sem, panel_sem, go,
     gathered, outgoing, incoming, solved, pivoted,
     row_send, row_recv, ring_send, ring_recv,
     part_send, part_recv, spread_send, spread_recv, pair_send, pair_recv, next_send, next_recv,
@@ -164,8 +176,15 @@
             if hop < hops(direction, quarter):
                 ring_step(direction, quarter, hop)
 
-    for direction, quarter in ORDER:
-        ring_start(direction, quarter, 0)
+    def ring_begin():
+        for direction, quarter in ORDER:
+            ring_start(direction, quarter, 0)
+
+    later = (r == 1) & (z < 4)
+
+    @pl.when(jnp.logical_not(later))
+    def _():
+        ring_begin()
 
     def pass_row(step, _):
         place = pl.ds(pl.multiple_of((step - 1) * CAP, CAP), CAP)
@@ -236,7 +255,7 @@
     def solve(k):
         for b in range(4):
             at = slice(b * PIECE, (b + 1) * PIECE)
-            x = dot(gathered[4 * k + b, at], pivoted[at])
+            x = dot3(gathered[4 * k + b, at], pivoted[at])
             solved[k * NB + b * PIECE : k * NB + (b + 1) * PIECE] = x
             if k == 0:
                 block_copy(b).start()
@@ -244,7 +263,7 @@
                 scatter(2 * k + b // 2)
             if b < 3:
                 rest = slice((b + 1) * PIECE, NB)
-                pivoted[rest] = pivoted[rest] - dot(gathered[4 * k + b, rest], x)
+                pivoted[rest] = pivoted[rest] - dot3(gathered[4 * k + b, rest], x)
         out_ref[...] = solved[k * NB : (k + 1) * NB]
         for b in range(4):
             if k == 0:
@@ -314,19 +333,31 @@
     def update(group):
         left_part = jnp.concatenate([gathered[2 * group], gathered[2 * group + 1]], axis=1)
         rows = pl.ds(pl.multiple_of(group * HALF, HALF), HALF)
-        pivoted[...] = pivoted[...] - dot(left_part, solved[rows])
+        pivoted[...] = pivoted[...] - dot3(left_part, solved[rows])
 
     @pl.when(r == 0)
     def _():
         for hop in range(4):
             ring_hop(hop, 0)
             ring_hop(hop, 1)
+            if hop == 0:
+                @pl.when(z < 4)
+                def _():
+                    pl.semaphore_signal(
+                        go, inc=1, device_id={"row": r + 1}, device_id_type=MESH
+                    )
+
             if hop == 1:
                 take_rows()
         solve(0)
 
     @pl.when(r == 1)
     def _():
+        @pl.when(later)
+        def _():
+            pl.semaphore_wait(go, 1)
+            ring_begin()
+
         for hop in range(4):
             ring_hop(hop, 0)
             ring_hop(hop, 1)
@@ -334,14 +365,13 @@
                 take_rows()
         for b in range(4):
             block_copy(b).wait_recv()
-            pivoted[...] = pivoted[...] - dot(
+            pivoted[...] = pivoted[...] - dot3(
                 gathered[b], solved[b * PIECE : (b + 1) * PIECE]
             )
         solve(1)
 
     @pl.when(r >= 2)
     def _():
-        last = lax.rem(z + COLS // 2, COLS) // 2
         ring_hop(0, 0)
         ring_hop(0, 1)
         take_rows()
@@ -358,23 +388,16 @@
         pair(2)
         ring_hop(3, 0)
         ring_hop(3, 1)
-        pair(3)
 
         def early(group, _):
             pair_copy(group).wait_recv()
-
-            @pl.when(group != last)
-            def _():
-                update(group)
-
+            update(group)
             return 0
 
-        lax.fori_loop(0, 3, early, 0)
-
-        @pl.when(last != 3)
-        def _():
-            update(last)
-
+        lax.fori_loop(0, 2, early, 0)
+        pair(3)
+        pair_copy(2).wait_recv()
+        update(2)
         pair_copy(3).wait_recv()
         update(3)
         out_ref[...] = pivoted[...]
@@ -403,6 +426,7 @@
         out_specs=vmem,
         scratch_shapes=[
             pltpu.VMEM(objective.shape, F32), pltpu.VMEM((1, NB), jnp.int32), dma, dma, dma,
+            pltpu.SemaphoreType.REGULAR,
             pltpu.VMEM((COLS, NB, PIECE), F32),
             pltpu.VMEM((HALF, width), F32),
             pltpu.VMEM((HALF, width), F32),

time: 46.5 us -> 44.2 us (0.951)
  the two profiles are of different devices: /device:TPU:196 before, /device:TPU:9 now
where the time goes in v4:
time: 44.2 us; the launch traced here: 44.1 us
  Pallas kernels  43.3 us (98%)
  local copies, waits for them, and re-layouts  0.8 us (2%)
    pallas_call x1, Pallas kernels, body(): pl.pallas_call(kernel, out_shape=jax.ShapeDtypeStruct(objective.shape, F3...  43.3 us

profile of v4, /device:TPU:9, one launch (start us, length us, event | category | flops | bytes accessed | tf_op | source)
XLA Modules:
  0.0 44.1 jit_solution(2681669505907348979)
XLA Ops:
  0.0 43.3 %zonal.1 = f32[512,256]{1,0:T(8,128)S(1)} custom-call(f32[512,256]{1,0:T(8,128)} %obj_hbm.1, s32[1,512]{1,0:T(1,128)} %bitcast.1, f32[512,128]{1,0:T(8,128)} %panel_hbm.1), custom_call_target="tpu_custom_call" | custom-call | tf_op jit(solution)/shard_map/zonal/pallas_call | solution.py:422
  43.3 0.8 %copy.5 = f32[512,256]{1,0:T(8,128)} copy(f32[512,256]{1,0:T(8,128)S(1)} %zonal.1) | data formatting | bytes 1048576

commit v5 on v4

--- a/solution.py
+++ b/solution.py
@@ -13,7 +13,7 @@
 COLS = 8
 HALF = NB // 2
 PART = HALF // CHIPS
-HELPER = 4
+HELPERS = (4, 12)
 F32 = jnp.float32
 BF16 = jnp.bfloat16
 MESH = pl.DeviceIdType.MESH
@@ -68,7 +68,7 @@
 
 def kernel(
     obj_hbm, piv_hbm, panel_hbm, out_ref,
-    obj_ref, piv_ref, obj_sem, piv_sem, panel_sem, go,
+    obj_ref, piv_ref, obj_sem, piv_sem, panel_sem, go, tile_high, tile_low,
     gathered, outgoing, incoming, solved, pivoted,
     row_send, row_recv, ring_send, ring_recv,
     part_send, part_recv, spread_send, spread_recv, pair_send, pair_recv, next_send, next_recv,
@@ -226,8 +226,18 @@
             device_id={"row": device}, device_id_type=MESH,
         )
 
+    def piece_copy(group, piece, half, send, recv, device):
+        place = solved.at[
+            pl.ds(pl.multiple_of(group * HALF + piece * 8, 8), 8),
+            pl.ds(pl.multiple_of(half * PIECE, PIECE), PIECE),
+        ]
+        return pltpu.make_async_remote_copy(
+            src_ref=place, dst_ref=place, send_sem=send.at[group], recv_sem=recv.at[group],
+            device_id={"row": device}, device_id_type=MESH,
+        )
+
     def parts(group, count, send, recv):
-        place = solved.at[pl.ds(0, count * PART), pl.ds(0, PIECE)]
+        place = solved.at[pl.ds(0, count * 8), pl.ds(0, PIECE)]
         return pltpu.make_async_remote_copy(
             src_ref=place, dst_ref=place, send_sem=send.at[group], recv_sem=recv.at[group],
             device_id=right, device_id_type=MESH,
@@ -250,7 +260,10 @@
 
         lax.fori_loop(2, ROWS, one, 0)
         for half in range(2):
-            part_copy(group, 0, half, part_send, part_recv, 2 * HELPER + half).start()
+            for piece in range(2):
+                piece_copy(
+                    group, piece, half, part_send, part_recv, 2 * HELPERS[piece] + half
+                ).start()
 
     def solve(k):
         for b in range(4):
@@ -275,27 +288,31 @@
                 recv_sem=part_recv.at[0], device_id=right, device_id_type=MESH,
             ).wait_send()
 
+    helps = (chip == HELPERS[0]) | (chip == HELPERS[1])
+
     def spread(group):
-        def pass_on(part):
-            def one(step, _):
-                other = lax.rem(chip - 1 + step, CHIPS - 1) + 1
-                part_copy(
-                    group, part, core, spread_send, spread_recv, other * 2 + core
+        @pl.when(helps)
+        def _():
+            parts(group, 3, part_send, part_recv).wait_recv()
+
+        @pl.when(jnp.logical_not(helps))
+        def _():
+            parts(group, 2, part_send, part_recv).wait_recv()
+
+        def one(step, _):
+            other = lax.rem(chip - 1 + step, CHIPS - 1) + 1
+            part_copy(group, chip, core, spread_send, spread_recv, other * 2 + core).start()
+
+            @pl.when(helps)
+            def _():
+                piece_copy(
+                    group, jnp.where(chip == HELPERS[0], 0, 1), core,
+                    spread_send, spread_recv, other * 2 + core,
                 ).start()
-                return 0
-
-            lax.fori_loop(1, CHIPS - 1, one, 0)
-
-        @pl.when(chip == HELPER)
-        def _():
-            parts(group, 2, part_send, part_recv).wait_recv()
-            pass_on(0)
-
-        @pl.when(chip != HELPER)
-        def _():
-            parts(group, 1, part_send, part_recv).wait_recv()
-
-        pass_on(chip)
+
+            return 0
+
+        lax.fori_loop(1, CHIPS - 1, one, 0)
 
     def pair_copy(group):
         place = solved.at[
@@ -309,24 +326,24 @@
         )
 
     def pair(group):
-        @pl.when(chip == HELPER)
-        def _():
-            parts(group, 14, spread_send, spread_recv).wait_recv()
-
-        @pl.when(chip != HELPER)
-        def _():
-            parts(group, 15, spread_send, spread_recv).wait_recv()
+        @pl.when(helps)
+        def _():
+            parts(group, 29, spread_send, spread_recv).wait_recv()
+
+        @pl.when(jnp.logical_not(helps))
+        def _():
+            parts(group, 30, spread_send, spread_recv).wait_recv()
 
         pair_copy(group).start()
 
     def passed(group):
-        @pl.when(chip == HELPER)
+        @pl.when(helps)
+        def _():
+            parts(group, 42, spread_send, spread_recv).wait_send()
+
+        @pl.when(jnp.logical_not(helps))
         def _():
             parts(group, 28, spread_send, spread_recv).wait_send()
-
-        @pl.when(chip != HELPER)
-        def _():
-            parts(group, 14, spread_send, spread_recv).wait_send()
 
         pair_copy(group).wait_send()
 
@@ -351,6 +368,13 @@
                 take_rows()
         solve(0)
 
+    def ring_kind(hop, below):
+        for direction, quarter in ORDER:
+            if hop < hops(direction, quarter):
+                @pl.when((shard_of(direction, hop + 1) < 4) == below)
+                def _():
+                    ring_step(direction, quarter, hop)
+
     @pl.when(r == 1)
     def _():
         @pl.when(later)
@@ -358,11 +382,14 @@
             pl.semaphore_wait(go, 1)
             ring_begin()
 
-        for hop in range(4):
-            ring_hop(hop, 0)
-            ring_hop(hop, 1)
-            if hop == 1:
+        for hop in range(5):
+            if hop < 4:
+                ring_kind(hop, False)
+            if hop >= 1:
+                ring_kind(hop - 1, True)
+            if hop == 2:
                 take_rows()
+
         for b in range(4):
             block_copy(b).wait_recv()
             pivoted[...] = pivoted[...] - dot3(
@@ -395,12 +422,24 @@
             return 0
 
         lax.fori_loop(0, 2, early, 0)
+        for k in range(2):
+            for b in range(2):
+                columns = slice(b * PIECE, (b + 1) * PIECE)
+                high, low = halves(gathered[4 + 2 * k + b])
+                tile_high[k, :, columns] = high
+                tile_low[k, :, columns] = low
+
+        def product(k):
+            high, low = halves(solved[(2 + k) * HALF : (3 + k) * HALF])
+            small = jnp.dot(tile_high[k], low, preferred_element_type=F32)
+            small = small + jnp.dot(tile_low[k], high, preferred_element_type=F32)
+            return small + jnp.dot(tile_high[k], high, preferred_element_type=F32)
+
         pair(3)
         pair_copy(2).wait_recv()
-        update(2)
+        pivoted[...] = pivoted[...] - product(0)
         pair_copy(3).wait_recv()
-        update(3)
-        out_ref[...] = pivoted[...]
+        out_ref[...] = pivoted[...] - product(1)
         for group in range(4):
             passed(group)
 
@@ -427,6 +466,7 @@
         scratch_shapes=[
             pltpu.VMEM(objective.shape, F32), pltpu.VMEM((1, NB), jnp.int32), dma, dma, dma,
             pltpu.SemaphoreType.REGULAR,
+            pltpu.VMEM((2, NB, HALF), BF16), pltpu.VMEM((2, NB, HALF), BF16),
             pltpu.VMEM((COLS, NB, PIECE), F32),
             pltpu.VMEM((HALF, width), F32),
             pltpu.VMEM((HALF, width), F32),

time: 44.2 us -> 44.1 us (level)
  no operation moved by 1% of the time
where the time goes in v5:
time: 44.1 us; the launch traced here: 44 us
  Pallas kernels  43.2 us (98%)
  local copies, waits for them, and re-layouts  0.8 us (2%)
    pallas_call x1, Pallas kernels, body(): pl.pallas_call(kernel, out_shape=jax.ShapeDtypeStruct(objective.shape, F3...  43.2 us

profile of v5, /device:TPU:9, one launch (start us, length us, event | category | flops | bytes accessed | tf_op | source)
XLA Modules:
  0.0 44.0 jit_solution(3188546410755876024)
XLA Ops:
  0.0 43.2 %zonal.1 = f32[512,256]{1,0:T(8,128)S(1)} custom-call(f32[512,256]{1,0:T(8,128)} %obj_hbm.1, s32[1,512]{1,0:T(1,128)} %bitcast.1, f32[512,128]{1,0:T(8,128)} %panel_hbm.1), custom_call_target="tpu_custom_call" | custom-call | tf_op jit(solution)/shard_map/zonal/pallas_call | solution.py:461
  43.3 0.8 %copy.5 = f32[512,256]{1,0:T(8,128)} copy(f32[512,256]{1,0:T(8,128)S(1)} %zonal.1) | data formatting | bytes 1048576
